TPU v7x, 32 devices: a whole 2x2x4 slice. The times are simulated.
32 devices in a mesh: dp: 8 (over z, y), head: 4 (over x, core).
Axes of the slice: x: 2, y: 2, z: 4, core: 2. Of those that a mesh axis runs over, the one named last changes fastest.
Arguments:
- hidden_in: bfloat16 [2048, 2048], P(('dp', 'head')), may hold values from -6 to 6
- norm_gain: bfloat16 [2048], replicated, may hold values from 0.25 to 1.75
- w_query: bfloat16 [2048, 2048], P(None, 'head'), may hold values from -0.125 to 0.125
- key_weight: bfloat16 [2048, 1024], P(None, 'head'), may hold values from -0.125 to 0.125
- w_value: bfloat16 [2048, 1024], P(None, 'head'), may hold values from -0.125 to 0.125
- query_gain: bfloat16 [128], replicated, may hold values from 0.796875 to 4
- key_gain: bfloat16 [128], replicated, may hold values from 0.25 to 1.75
- w_out: bfloat16 [2048, 2048], P('head'), may hold values from -0.125 to 0.125
- prefix_root_keys: bfloat16 [1024, 1024], P('dp', 'head'), may hold values from -210 to 210
- prefix_root_values: bfloat16 [1024, 1024], P('dp', 'head'), may hold values from -6 to 6
- mid_keys: bfloat16 [4096, 1024], P('dp', 'head'), may hold values from -210 to 210
- mid_values: bfloat16 [4096, 1024], P('dp', 'head'), may hold values from -6 to 6
- mid_lengths: int32 [16], replicated, may hold values from 1 to 256, 2048 in all
- leaf_keys: bfloat16 [4096, 1024], P('dp', 'head'), may hold values from -6 to 6
- leaf_values: bfloat16 [4096, 1024], P('dp', 'head'), may hold values from -6 to 6
- leaf_lengths: int32 [64], P('dp'), may hold values from 1 to 64, 2048 in all
- token_request: int32 [8, 256], P('dp'), may hold values from 0 to 7, never falling along the last dimension, each value on 1 to 64 neighbouring positions
- request_node: int32 [8, 8], P('dp'), may hold values from 0 to 15, as said below
Outputs:
- attn_update: bfloat16 [2048, 2048], P(('dp', 'head'))
- cache_keys: bfloat16 [2048, 1024], P('dp', 'head')
- cache_values: bfloat16 [2048, 1024], P('dp', 'head')
Inputs may be any that keep to these rules, and one draw needn't show every extreme that they name: `token_request`: in each row requests 0 to 7 all occur, in rising order, each on 1 to 64 consecutive tokens; some request has exactly 64. `request_node`: node v is held by dp index v // 2; the 8 requests of one row have parents on 8 different dp indices, one each.
All inputs are finite; a program needn't handle non-finite values. No bound on the sum of `leaf_lengths` on one device may be relied on, other than what follows from the above.
Results may differ from a plain program's by a relative error of at most 0.039.
Values may be sent and summed in bfloat16 or wider, within the bound.
A program may use at most 128 MiB of HBM per device.

v0:
```python
import math
import jax
import jax.numpy as jnp
from jax import lax
from jax.sharding import PartitionSpec as P

MID_DEV = 2
MID_LEN = 256
EPS = 1e-06
THETA = 1000000.0
MASKED = -1e30


def rms_rows(values, gain):
    power = jnp.mean(values * values, axis=-1, keepdims=True)
    return values * lax.rsqrt(power + EPS) * gain


def rotate(values, positions):
    width = values.shape[-1]
    half = width // 2
    exponent = jnp.arange(half).astype(jnp.float32) * (2.0 / width)
    freqs = jnp.power(THETA, -exponent)
    angles = positions.astype(jnp.float32)[:, None] * freqs[None, :]
    cosine = jnp.cos(angles)[:, None, :]
    sine = jnp.sin(angles)[:, None, :]
    first = values[..., :half]
    second = values[..., half:]
    return jnp.concatenate(
        [first * cosine - second * sine, second * cosine + first * sine], axis=-1
    )


def body(
    hidden_in,
    norm_gain,
    w_query,
    key_weight,
    w_value,
    query_gain,
    key_gain,
    w_out,
    prefix_root_keys,
    prefix_root_values,
    mid_keys,
    mid_values,
    mid_lengths,
    leaf_keys,
    leaf_values,
    leaf_lengths,
    token_request,
    request_node,
):
    head_dim = query_gain.shape[0]
    query_width = w_query.shape[1]
    key_width = key_weight.shape[1]
    kv_heads = key_width // head_dim
    query_group = query_width // key_width
    scale = 1.0 / math.sqrt(head_dim)
    dp_count = lax.axis_size("dp")
    normalized_input = rms_rows(
        hidden_in.astype(jnp.float32), norm_gain.astype(jnp.float32)
    ).astype(jnp.bfloat16)
    piece = lax.all_gather(normalized_input, "head", axis=0, tiled=True)
    mixed = jnp.concatenate(
        [
            jnp.dot(piece, w_query, preferred_element_type=jnp.float32),
            jnp.dot(piece, key_weight, preferred_element_type=jnp.float32),
            jnp.dot(piece, w_value, preferred_element_type=jnp.float32),
        ],
        axis=1,
    )
    height = mixed.shape[0]
    segment = token_request[0]
    branch_nodes = request_node[0]
    requests = branch_nodes.shape[0]
    request_ids = jnp.arange(requests, dtype=jnp.int32)
    token_ids = jnp.arange(height, dtype=jnp.int32)
    member = segment[None, :] == request_ids[:, None]
    counts = jnp.sum(member.astype(jnp.int32), axis=1)
    earlier = request_ids[None, :] < request_ids[:, None]
    starts = jnp.sum(jnp.where(earlier, counts[None, :], 0), axis=1)
    offset = token_ids - jnp.sum(jnp.where(member, starts[:, None], 0), axis=0)
    node_total = mid_lengths.shape[0]
    node_match = branch_nodes[:, None] == jnp.arange(node_total, dtype=jnp.int32)[None, :]
    branch_length = jnp.sum(jnp.where(node_match, mid_lengths[None, :], 0), axis=1)
    root_total = prefix_root_keys.shape[0] * dp_count
    positions = (
        root_total
        + jnp.sum(jnp.where(member, (branch_length + leaf_lengths)[:, None], 0), axis=0)
        + offset
    )
    query_part = mixed[:, :query_width].reshape(height, query_width // head_dim, head_dim)
    key_portion = mixed[:, query_width : query_width + key_width].reshape(
        height, kv_heads, head_dim
    )
    query_matrix = rotate(rms_rows(query_part, query_gain.astype(jnp.float32)), positions).astype(
        jnp.bfloat16
    )
    new_keys = rotate(rms_rows(key_portion, key_gain.astype(jnp.float32)), positions).astype(
        jnp.bfloat16
    )
    new_values = mixed[:, query_width + key_width :].astype(jnp.bfloat16)
    heads_query = query_matrix.reshape(height, kv_heads, query_group, head_dim)
    root_keys = lax.all_gather(prefix_root_keys, "dp", axis=0, tiled=True)
    root_values = lax.all_gather(prefix_root_values, "dp", axis=0, tiled=True)
    owner_of = branch_nodes // MID_DEV
    owner_ids = jnp.arange(dp_count, dtype=jnp.int32)
    owner_match = owner_of[None, :] == owner_ids[:, None]
    block_slot = jnp.sum(jnp.where(owner_match, (branch_nodes % MID_DEV)[None, :], 0), axis=1)
    block_request = jnp.sum(jnp.where(owner_match, request_ids[None, :], 0), axis=1)
    block_length = jnp.sum(jnp.where(owner_match, branch_length[None, :], 0), axis=1)
    wanted = lax.all_to_all(block_slot[:, None], "dp", split_axis=0, concat_axis=0, tiled=True)[
        :, 0
    ]
    second = (wanted == 1)[:, None, None]
    own_pairs = jnp.concatenate([mid_keys, mid_values], axis=1).reshape(
        MID_DEV, MID_LEN, 2 * key_width
    )
    sent = jnp.where(second, own_pairs[1][None], own_pairs[0][None])
    got = lax.all_to_all(sent, "dp", split_axis=0, concat_axis=0, tiled=True)
    got = got.reshape(dp_count * MID_LEN, 2 * key_width)
    leaf_each = leaf_keys.shape[0] // requests
    leaf_live = jnp.arange(leaf_each, dtype=jnp.int32)[None, :] < leaf_lengths[:, None]
    leaf_tag = jnp.where(leaf_live, request_ids[:, None], -1).reshape(-1)
    mid_live = jnp.arange(MID_LEN, dtype=jnp.int32)[None, :] < block_length[:, None]
    mid_tag = jnp.where(mid_live, block_request[:, None], -1).reshape(-1)
    own_mask = (segment[None, :] == segment[:, None]) & (token_ids[None, :] <= token_ids[:, None])
    mask = jnp.concatenate(
        [
            jnp.ones((height, root_keys.shape[0]), jnp.bool_),
            leaf_tag[None, :] == segment[:, None],
            own_mask,
            mid_tag[None, :] == segment[:, None],
        ],
        axis=1,
    )
    all_keys = jnp.concatenate(
        [root_keys, leaf_keys, new_keys.reshape(height, key_width), got[:, :key_width]], axis=0
    ).reshape(-1, kv_heads, head_dim)
    all_values = jnp.concatenate(
        [root_values, leaf_values, new_values, got[:, key_width:]], axis=0
    ).reshape(-1, kv_heads, head_dim)
    scores = jnp.einsum("tkgd,skd->kgts", heads_query, all_keys, preferred_element_type=jnp.float32)
    scores = jnp.where(mask[None, None], scores * scale, MASKED)
    weights = jnp.exp(scores - jnp.max(scores, axis=-1, keepdims=True))
    total = jnp.sum(weights, axis=-1)
    summed = jnp.einsum(
        "kgts,skd->kgtd",
        weights.astype(jnp.bfloat16),
        all_values,
        preferred_element_type=jnp.float32,
    )
    attn = (summed / total[..., None]).astype(jnp.bfloat16)
    attn = attn.transpose(2, 0, 1, 3).reshape(height, query_width)
    update = lax.psum_scatter(
        jnp.dot(attn, w_out, preferred_element_type=jnp.float32).astype(jnp.bfloat16),
        "head",
        scatter_dimension=0,
        tiled=True,
    )
    return (update, new_keys.reshape(height, key_width), new_values)


def solution(mesh):
    in_specs = (
        P(("dp", "head"), None),
        P(),
        P(None, "head"),
        P(None, "head"),
        P(None, "head"),
        P(),
        P(),
        P("head", None),
        P("dp", "head"),
        P("dp", "head"),
        P("dp", "head"),
        P("dp", "head"),
        P(),
        P("dp", "head"),
        P("dp", "head"),
        P("dp"),
        P("dp", None),
        P("dp", None),
    )
    out_specs = (P(("dp", "head"), None), P("dp", "head"), P("dp", "head"))
    return jax.shard_map(body, mesh=mesh, in_specs=in_specs, out_specs=out_specs, check_vma=False)
```

profile of v0, /device:TPU:0, one launch (start us, length us, event | category | flops | bytes accessed | tf_op | source)
XLA Modules:
  0.0 206.7 jit_solution(16049318135466380190)
XLA Ops:
  7.2 0.8 fusion.29
  8.0 0.9 select_reduce_fusion.6
  9.7 7.3 %all-to-all-start = ((s32[8,1,1]{2,1,0:T(1,128)}), s32[8,1,1]{2,1,0:T(1,128)S(1)}, u32[]{:S(2)}, u32[]{:S(2)}) async-start(s32[8,1,1]{2,1,0:T(1,128)} %copy.122), calls=%async_computation | async-start | bytes 8192 | tf_op jit(solution)/shard_map/all_to_all | solution.py:113
  17.7 1.1 fusion.22
  18.8 1.8 fusion.24
  22.1 1.0 constant_dynamic-update-slice_fusion.1
  23.0 1.0 constant_dynamic-update-slice_fusion
  24.0 0.8 fusion.35
  24.8 1.0 copy.133
  25.8 29.8 %all_gather.11 = bf16[1024,256]{0,1:T(8,128)(2,1)} all-gather(bf16[128,256]{0,1:T(8,128)(2,1)S(1)} %copy.133), channel_id=1, replica_groups=mesh['dp'=8,'head'=4] {'dp'}, dimensions={0}, use_global_device_ids=true | all-gather | bytes 589824 | tf_op jit(solution)/shard_map/all_gather | solution.py:106
  56.5 27.1 %all_gather.9 = bf16[1024,256]{0,1:T(8,128)(2,1)S(1)} all-gather(bf16[128,256]{0,1:T(8,128)(2,1)S(1)} %copy.119), channel_id=1, replica_groups=mesh['dp'=8,'head'=4] {'dp'}, dimensions={0}, use_global_device_ids=true | all-gather | bytes 589824 | tf_op jit(solution)/shard_map/all_gather | solution.py:105
  84.4 1.8 copy.124
  86.2 1.8 copy.123
  88.0 1.8 copy.134
  91.1 1.8 copy.120
  92.9 1.8 copy.127
  94.7 1.0 copy.126
  96.0 2.7 %broadcast_select_fusion = bf16[8,256,512]{1,2,0:T(8,128)(2,1)} fusion(pred[8]{0:T(512)(128)(4,1)S(1)} %compare_reduce_fusion, bf16[256,512]{0,1:T(8,128)(2,1)} %copy.124, bf16[256,512]{0,1:T(8,128)(2,1)} %copy.123), kind=kLoop, calls=%fused_computation.9 | loop fusion | flops 1048576 | bytes 2621448 | tf_op jit(solution)/shard_map/jit(_where)/select_n | solution.py:120
  98.6 4.4 %all-to-all-start.1 = ((bf16[8,256,512]{1,2,0:T(8,128)(2,1)}), bf16[8,256,512]{1,2,0:T(8,128)(2,1)}, u32[]{:S(2)}, u32[]{:S(2)}) async-start(bf16[8,256,512]{1,2,0:T(8,128)(2,1)} %broadcast_select_fusion), calls=%async_computation.1 | async-start | bytes 4194304 | tf_op jit(solution)/shard_map/all_to_all | solution.py:121
  103.2 7.0 %pad_add_fusion = pred[256,3840]{0,1:T(8,128)(4,1)} fusion(pred[256,2048]{0,1:T(8,128)(4,1)S(1)} %broadcast_compare_fusion, pred[256,256]{0,1:T(8,128)(4,1)S(1)} %fusion.28, pred[256,512]{0,1:T(8,128)(4,1)S(1)} %broadcast_compare_fusion.1, pred[3840]{0:T(1024)(128)(4,1)S(1)} %pad.8.clone), kind=kLoop, calls=%fused_computation.7 | loop fusion | flops 2949120 | bytes 1707776 | tf_op jit(solution)/shard_map/concatenate | solution.py:129
  110.2 2.0 convolution_convert_fusion.1
  112.9 2.6 %fusion.36 = f32[256,512]{1,0:T(8,128)S(1)} fusion(bf16[256,2048]{1,0:T(8,128)(2,1)} %all-gather.2.cloned.1.call-done, bf16[2048,512]{1,0:T(8,128)(2,1)} %param.20), kind=kOutput, calls=%fused_computation.82 | convolution fusion | flops 536870912 | bytes 3670016 | tf_op jit(solution)/shard_map/dot_general | solution.py:67
  119.6 22.3 %all-to-all-done.1 = bf16[8,256,512]{1,2,0:T(8,128)(2,1)} async-done(((bf16[8,256,512]{1,2,0:T(8,128)(2,1)}), bf16[8,256,512]{1,2,0:T(8,128)(2,1)}, u32[]{:S(2)}, u32[]{:S(2)}) %all-to-all-start.1) | async-done | bytes 2097184 | tf_op jit(solution)/shard_map/all_to_all | solution.py:121
  141.9 1.9 copy.142
  143.8 1.1 fusion.34
  145.0 1.3 copy.128
  146.3 10.1 %fusion.2 = (f32[2,2,256]{2,1,0:T(2,128)S(1)}, f32[2,3840,256,2]{2,1,3,0:T(8,128)}) fusion(pred[256,3840]{0,1:T(8,128)(4,1)} %pad_add_fusion, bf16[256,2,2,64]{3,0,2,1:T(8,128)(2,1)} %bitcast.71, bf16[256,2,2,64]{3,0,2,1:T(8,128)(2,1)} %bitcast.72, bf16[2048,2,128]{2,0,1:T(8,128)(2,1)} %copy.128, bf16[256,2,128]{2,0,1:T(8,128)(2,1)S(1)} %maximum_convert_fusion, ...), kind=kOutput, calls=%fused_computation.4 | convolution fusion | flops 1026817024 | bytes 18944000 | tf_op jit(solution)/shard_map/tkgd,skd->kgts/dot_general | solution.py:144
  156.4 9.1 %fusion = f32[2,2,256]{2,1,0:T(2,128)S(1)} fusion(f32[2,3840,256,2]{2,1,3,0:T(8,128)} %get-tuple-element.41, f32[2,2,256]{2,1,0:T(2,128)S(1)} %get-tuple-element.40, pred[256,3840]{0,1:T(8,128)(4,1)} %pad_add_fusion), kind=kLoop, calls=%fused_computation.2 | loop fusion | flops 15727616 | bytes 16719872 | tf_op jit(solution)/shard_map/reduce_sum | solution.py:147
  165.5 1.2 pad_maximum_fusion
  166.8 7.7 %fusion.19 = bf16[256,2,2,128]{0,3,2,1:T(8,128)(2,1)S(1)} fusion(bf16[3840,2,128,1]{0,2,3,1:T(8,128)(2,1)S(1)} %bitcast.67, f32[2,3840,256,2]{2,1,3,0:T(8,128)} %get-tuple-element.41, f32[2,2,256]{2,1,0:T(2,128)S(1)} %get-tuple-element.40, pred[256,3840]{0,1:T(8,128)(4,1)S(1)} %copy-done.3, f32[256,2,2]{0,2,1:T(2,128)S(1)} %bitcast.80), kind=kOutput, calls=%fused_computation.22 | convolution fusion | flops 1022623744 | bytes 18948096 | tf_op jit(solution)/shard_map/kgts,skd->kgtd/dot_general | solution.py:148
  174.5 1.7 convolution_convert_fusion
  177.2 22.7 %reduce-scatter.2.cloned.1.call-done = bf16[64,2048]{1,0:T(8,128)(2,1)} async-done(((bf16[256,2048]{1,0:T(8,128)(2,1)}), bf16[64,2048]{1,0:T(8,128)(2,1)}) %reduce-scatter.2.cloned.1.call-update) | async-done | bytes 262160 | tf_op jit(solution)/shard_map/reduce_scatter | solution.py:156
  (72 shorter events, 12.2 us)
Async XLA Ops:
  7.2 167.4 %copy-start = (bf16[512,2048]{1,0:T(8,128)(2,1)S(1)}, bf16[512,2048]{1,0:T(8,128)(2,1)}, u32[]{:S(2)}) copy-start(bf16[512,2048]{1,0:T(8,128)(2,1)} %param.25) | copy-start | bytes 6291460
  7.2 48.5 %copy-start.12 = (s32[1,256]{1,0:T(1,128)S(1)}, s32[1,256]{1,0:T(1,128)}, u32[]{:S(2)}) copy-start(s32[1,256]{1,0:T(1,128)} %param.34) | copy-start | bytes 3076
  7.2 49.2 %copy-start.11 = (bf16[128,256]{1,0:T(8,128)(2,1)S(1)}, bf16[128,256]{1,0:T(8,128)(2,1)}, u32[]{:S(2)}) copy-start(bf16[128,256]{1,0:T(8,128)(2,1)} %param.26) | copy-start | bytes 196612
  9.7 86.0 %all-to-all-start = ((s32[8,1,1]{2,1,0:T(1,128)}), s32[8,1,1]{2,1,0:T(1,128)S(1)}, u32[]{:S(2)}, u32[]{:S(2)}) async-start(s32[8,1,1]{2,1,0:T(1,128)} %copy.122), calls=%async_computation | async-start | bytes 8192 | tf_op jit(solution)/shard_map/all_to_all | solution.py:113
  17.0 93.2 %all-gather.2.cloned.1.call-start = ((), (), s32[]{:S(2)}) async-start(), calls=%async_computation.3 | async-start | bytes 1310720 | tf_op jit(solution)/shard_map/all_gather | solution.py:64
  98.6 43.3 %all-to-all-start.1 = ((bf16[8,256,512]{1,2,0:T(8,128)(2,1)}), bf16[8,256,512]{1,2,0:T(8,128)(2,1)}, u32[]{:S(2)}, u32[]{:S(2)}) async-start(bf16[8,256,512]{1,2,0:T(8,128)(2,1)} %broadcast_select_fusion), calls=%async_computation.1 | async-start | bytes 4194304 | tf_op jit(solution)/shard_map/all_to_all | solution.py:121
  103.0 96.9 %reduce-scatter.2.cloned.1.call-start = ((), (), s32[]{:S(2)}) async-start(), calls=%async_computation.4 | async-start | bytes 1310720 | tf_op jit(solution)/shard_map/reduce_scatter | solution.py:156
  112.1 4.9 %copy-start.6 = (bf16[256,256]{1,0:T(8,128)(2,1)}, bf16[256,256]{1,0:T(8,128)(2,1)S(1)}, u32[]{:S(2)}) copy-start(bf16[256,256]{1,0:T(8,128)(2,1)S(1)} %convolution_convert_fusion.1) | copy-start | bytes 393220
  115.7 2.8 %copy-start.1 = (bf16[256,2048]{1,0:T(8,128)(2,1)S(1)}, bf16[256,2048]{1,0:T(8,128)(2,1)}, u32[]{:S(2)}) copy-start(bf16[256,2048]{1,0:T(8,128)(2,1)} %all-gather.2.cloned.1.call-done) | copy-start | bytes 3145732
  115.7 2.8 %copy-start.4 = (bf16[2048,256]{1,0:T(8,128)(2,1)S(1)}, bf16[2048,256]{1,0:T(8,128)(2,1)}, u32[]{:S(2)}) copy-start(bf16[2048,256]{1,0:T(8,128)(2,1)} %param.21) | copy-start | bytes 3145732
  119.6 26.7 %copy-start.8 = (bf16[256,2,128]{2,0,1:T(8,128)(2,1)}, bf16[256,2,128]{2,0,1:T(8,128)(2,1)S(1)}, u32[]{:S(2)}) copy-start(bf16[256,2,128]{2,0,1:T(8,128)(2,1)S(1)} %maximum_convert_fusion) | copy-start | bytes 393220
  143.8 2.5 %copy-start.10 = (bf16[512,2,128]{2,0,1:T(8,128)(2,1)S(1)}, bf16[512,2,128]{2,0,1:T(8,128)(2,1)}, u32[]{:S(2)}) copy-start(bf16[512,2,128]{2,0,1:T(8,128)(2,1)} %copy.127) | copy-start | bytes 786436
  156.3 9.1 %copy-start.2 = (bf16[2048,256]{0,1:T(8,128)(2,1)S(1)}, bf16[2048,256]{0,1:T(8,128)(2,1)}, u32[]{:S(2)}) copy-start(bf16[2048,256]{0,1:T(8,128)(2,1)} %get-tuple-element.27) | copy-start | bytes 3145732
  156.3 9.1 %copy-start.5 = (bf16[512,256]{0,1:T(8,128)(2,1)S(1)}, bf16[512,256]{0,1:T(8,128)(2,1)}, u32[]{:S(2)}) copy-start(bf16[512,256]{0,1:T(8,128)(2,1)} %copy.134) | copy-start | bytes 786436
  156.3 9.1 %copy-start.7 = (bf16[256,256]{0,1:T(8,128)(2,1)S(1)}, bf16[256,256]{0,1:T(8,128)(2,1)}, u32[]{:S(2)}) copy-start(bf16[256,256]{0,1:T(8,128)(2,1)} %copy.135) | copy-start | bytes 393220
  165.4 1.4 copy-start.3
  174.5 1.8 copy-start.9
Sparse Core Ops, SparseCore 0:
  20.8 18.0 all-gather.1
  176.4 23.4 reduce-scatter.1
where the time goes:
time: 208 us; the launch traced here: 207 us
  blocking collectives  56.8 us (27%)
  waiting for transfers between devices  45.1 us (22%)
  other arithmetic  31.6 us (15%)
  matrix products  24.6 us (12%)
  local copies, waits for them, and re-layouts  22.5 us (11%)
  between operations  14.4 us (7%)
  starting transfers between devices  11.7 us (6%)
    all_gather x1, blocking collectives, body(): root_values = lax.all_gather(prefix_root_values, 'dp', axis=0, tiled=True)  29.8 us
    all_gather x1, blocking collectives, body(): root_keys = lax.all_gather(prefix_root_keys, 'dp', axis=0, tiled=True)  27.1 us
    reduce_scatter x1, waiting for transfers between devices, body(): lax.psum_scatter(jnp.dot(attn, w_out, preferred_element_type=jnp.float32)...  22.7 us
    all_to_all x1, waiting for transfers between devices, body(): got = lax.all_to_all(sent, 'dp', split_axis=0, concat_axis=0, tiled=True)  22.3 us
    dot_general x1, matrix products, body(): jnp.einsum('tkgd,skd->kgts', heads_query, all_keys, preferred_element_typ...  10.1 us
    reduce_sum x1, other arithmetic, body(): total = jnp.sum(weights, axis=-1)  9.09 us
    dot_general x1, matrix products, body(): jnp.einsum('kgts,skd->kgtd', weights.astype(jnp.bfloat16), all_values, pr...  7.7 us
    all_to_all x1, starting transfers between devices, body(): lax.all_to_all(block_slot[:, None], 'dp', split_axis=0, concat_axis=0, ti...  7.28 us
  transfers between devices with their start and end apart: 4, of which 2 were waited for; matrix products, arithmetic and copies ran while one was open for 20% of the time, Pallas kernels for 0%

commit v1 on v0

--- a/solution.py
+++ b/solution.py
@@ -9,6 +9,27 @@
 EPS = 1e-06
 THETA = 1000000.0
 MASKED = -1e30
+
+
+def collect(x, axis, dim):
+    size, mine, width = (lax.axis_size(axis), lax.axis_index(axis), x.shape[dim])
+    right = [(i, (i + 1) % size) for i in range(size)]
+    left = [(i, (i - 1) % size) for i in range(size)]
+    out = jnp.zeros((*x.shape[:dim], size * width, *x.shape[dim + 1 :]), x.dtype)
+    out = lax.dynamic_update_slice_in_dim(out, x, mine * width, axis=dim)
+    from_left = from_right = x
+    halfway = size // 2
+    for step in range(1, halfway + 1):
+        from_left = lax.ppermute(from_left, axis, right)
+        out = lax.dynamic_update_slice_in_dim(
+            out, from_left, (mine - step) % size * width, axis=dim
+        )
+        if step < size - halfway:
+            from_right = lax.ppermute(from_right, axis, left)
+            out = lax.dynamic_update_slice_in_dim(
+                out, from_right, (mine + step) % size * width, axis=dim
+            )
+    return out
 
 
 def rms_rows(values, gain):
@@ -103,7 +124,7 @@
     new_values = mixed[:, query_width + key_width :].astype(jnp.bfloat16)
     heads_query = query_matrix.reshape(height, kv_heads, query_group, head_dim)
     root_keys = lax.all_gather(prefix_root_keys, "dp", axis=0, tiled=True)
-    root_values = lax.all_gather(prefix_root_values, "dp", axis=0, tiled=True)
+    root_values = collect(prefix_root_values, "dp", 0)
     owner_of = branch_nodes // MID_DEV
     owner_ids = jnp.arange(dp_count, dtype=jnp.int32)
     owner_match = owner_of[None, :] == owner_ids[:, None]

time: 208 us -> 215 us (1.034)
  blocking collectives: 56.8 us -> 28.7 us
  waiting for transfers between devices: 45.1 us -> 59.3 us
  starting transfers between devices: 11.7 us -> 23.2 us
  local copies, waits for them, and re-layouts: 22.5 us -> 29.3 us
    ppermute x0 -> x7, waiting for transfers between devices: none -> 32.1 us  [the longest x4 32.1 us: collect(): from_left = lax.ppermute(from_left, axis, right)]
    all_gather x1 -> x0, blocking collectives: 29.8 us -> none  [body(): root_values = lax.all_gather(prefix_root_values, 'dp', axis=0, tiled=True)]
    all_to_all x1, waiting for transfers between devices: 22.3 us -> 0.01 us  [body(): got = lax.all_to_all(sent, 'dp', split_axis=0, concat_axis=0, tiled=True)]
    ppermute x0 -> x7, starting transfers between devices: none -> 15.5 us  [the longest x3 10.6 us: collect(): from_right = lax.ppermute(from_right, axis, left)]
    dynamic_update_slice x0 -> x8, local copies, waits for them, and re-layouts: none -> 7.64 us  [the longest x4 3.39 us: collect(): lax.dynamic_update_slice_in_dim(out, from_left, (mine - step) % size * wi...]
    reduce_scatter x1, waiting for transfers between devices: 22.7 us -> 27.2 us  [body(): lax.psum_scatter(jnp.dot(attn, w_out, preferred_element_type=jnp.float32)...]
    all_to_all x1, starting transfers between devices: 7.28 us -> 3.3 us  [body(): lax.all_to_all(block_slot[:, None], 'dp', split_axis=0, concat_axis=0, ti...]
    unnamed x33 -> x29, local copies, waits for them, and re-layouts: 6.52 us -> 6.49 us
  transfers between devices with their start and end apart: 4 -> 11, of which waited for: 2 -> 4; matrix products, arithmetic and copies ran while one was open for 20% -> 24% of each run, Pallas kernels for 0% -> 0%
where the time goes in v1:
time: 215 us; the launch traced here: 214 us
  waiting for transfers between devices  59.3 us (28%)
  other arithmetic  33.5 us (16%)
  local copies, waits for them, and re-layouts  29.3 us (14%)
  blocking collectives  28.7 us (13%)
  matrix products  25.5 us (12%)
  starting transfers between devices  23.2 us (11%)
  between operations  14.4 us (7%)
    ppermute x4, waiting for transfers between devices, collect(): from_left = lax.ppermute(from_left, axis, right)  32.1 us
    all_gather x1, blocking collectives, body(): root_keys = lax.all_gather(prefix_root_keys, 'dp', axis=0, tiled=True)  28.7 us
    reduce_scatter x1, waiting for transfers between devices, body(): lax.psum_scatter(jnp.dot(attn, w_out, preferred_element_type=jnp.float32)...  27.2 us
    ppermute x3, starting transfers between devices, collect(): from_right = lax.ppermute(from_right, axis, left)  10.6 us
    dot_general x1, matrix products, body(): jnp.einsum('tkgd,skd->kgts', heads_query, all_keys, preferred_element_typ...  10.2 us
    reduce_sum x1, other arithmetic, body(): total = jnp.sum(weights, axis=-1)  9.08 us
    dot_general x1, matrix products, body(): jnp.einsum('kgts,skd->kgtd', weights.astype(jnp.bfloat16), all_values, pr...  7.7 us
    unnamed x29, local copies, waits for them, and re-layouts  6.49 us
  transfers between devices with their start and end apart: 11, of which 4 were waited for; matrix products, arithmetic and copies ran while one was open for 24% of the time, Pallas kernels for 0%

profile of v1, /device:TPU:0, one launch (start us, length us, event | category | flops | bytes accessed | tf_op | source)
XLA Modules:
  0.0 213.8 jit_solution(15094773405789218817)
XLA Ops:
  7.2 1.7 copy.150
  8.9 3.0 %collective-permute-start = (bf16[128,256]{0,1:T(8,128)(2,1)}, bf16[128,256]{0,1:T(8,128)(2,1)}, u32[]{:S(2)}, u32[]{:S(2)}) collective-permute-start(bf16[128,256]{0,1:T(8,128)(2,1)} %copy.150), channel_id=1, source_target_pairs={{0,4},{4,8},{8,12},{12,16},{16,20},{20,24},{24,28},{28,0},{1,5},{5... | collective-permute-start | bytes 196616 | tf_op jit(solution)/shard_map/ppermute | solution.py:23
  11.9 3.0 %collective-permute-start.1 = (bf16[128,256]{0,1:T(8,128)(2,1)}, bf16[128,256]{0,1:T(8,128)(2,1)}, u32[]{:S(2)}, u32[]{:S(2)}) collective-permute-start(bf16[128,256]{0,1:T(8,128)(2,1)} %copy.150), channel_id=1, source_target_pairs={{0,28},{4,0},{8,4},{12,8},{16,12},{20,16},{24,20},{28,24},{1,29},{... | collective-permute-start | bytes 196616 | tf_op jit(solution)/shard_map/ppermute | solution.py:28
  17.3 3.3 %all-to-all-start = ((s32[8,1,1]{2,1,0:T(1,128)}), s32[8,1,1]{2,1,0:T(1,128)S(1)}, u32[]{:S(2)}, u32[]{:S(2)}) async-start(s32[8,1,1]{2,1,0:T(1,128)} %copy.139), calls=%async_computation | async-start | bytes 8192 | tf_op jit(solution)/shard_map/all_to_all | solution.py:134
  21.3 1.1 fusion.22
  22.4 1.8 fusion.24
  25.6 1.5 fusion.28
  30.7 1.1 broadcast_compare_fusion
  32.9 28.7 %all_gather.6 = bf16[1024,256]{0,1:T(8,128)(2,1)S(1)} all-gather(bf16[128,256]{0,1:T(8,128)(2,1)} %copy.136), channel_id=1, replica_groups=mesh['dp'=8,'head'=4] {'dp'}, dimensions={0}, use_global_device_ids=true | all-gather | bytes 589824 | tf_op jit(solution)/shard_map/all_gather | solution.py:126
  61.7 6.4 %pad_add_fusion = pred[256,3840]{0,1:T(8,128)(4,1)} fusion(pred[256,2048]{0,1:T(8,128)(4,1)S(1)} %broadcast_compare_fusion, pred[256,256]{0,1:T(8,128)(4,1)} %fusion.28, pred[256,512]{0,1:T(8,128)(4,1)S(1)} %broadcast_compare_fusion.1, pred[3840]{0:T(1024)(128)(4,1)S(1)} %pad.8.clone), kind=kLoop, calls=%fused_computation.7 | loop fusion | flops 2949120 | bytes 1707776 | tf_op jit(solution)/shard_map/concatenate | solution.py:150
  75.6 2.5 %broadcast_select_fusion = bf16[8,256,512]{1,2,0:T(8,128)(2,1)} fusion(pred[8]{0:T(512)(128)(4,1)S(1)} %compare_reduce_fusion, bf16[256,512]{0,1:T(8,128)(2,1)S(1)} %copy.141, bf16[256,512]{0,1:T(8,128)(2,1)} %copy.140), kind=kLoop, calls=%fused_computation.9 | loop fusion | flops 1048576 | bytes 2621448 | tf_op jit(solution)/shard_map/jit(_where)/select_n | solution.py:141
  78.1 4.3 %all-to-all-start.1 = ((bf16[8,256,512]{1,2,0:T(8,128)(2,1)}), bf16[8,256,512]{1,2,0:T(8,128)(2,1)}, u32[]{:S(2)}, u32[]{:S(2)}) async-start(bf16[8,256,512]{1,2,0:T(8,128)(2,1)} %broadcast_select_fusion), calls=%async_computation.1 | async-start | bytes 4194304 | tf_op jit(solution)/shard_map/all_to_all | solution.py:142
  83.9 1.5 constant_dynamic-update-slice_fusion.8
  85.4 1.9 collective-permute-start.2
  87.3 2.9 %collective-permute-start.3 = (bf16[128,256]{0,1:T(8,128)(2,1)}, bf16[128,256]{0,1:T(8,128)(2,1)S(1)}, u32[]{:S(2)}, u32[]{:S(2)}) collective-permute-start(bf16[128,256]{0,1:T(8,128)(2,1)} %collective-permute-done.1), channel_id=1, source_target_pairs={{0,28},{4,0},{8,4},{12,8},{16,12},{20,16},{24,20},{28,24},{1,29},{... | collective-permute-start | bytes 196616 | tf_op jit(solution)/shard_map/ppermute | solution.py:28
  90.1 1.5 constant_dynamic-update-slice_fusion.7
  91.6 1.5 constant_dynamic-update-slice_fusion.6
  93.1 25.4 %collective-permute-done.2 = bf16[128,256]{0,1:T(8,128)(2,1)S(1)} collective-permute-done((bf16[128,256]{0,1:T(8,128)(2,1)}, bf16[128,256]{0,1:T(8,128)(2,1)S(1)}, u32[]{:S(2)}, u32[]{:S(2)}) %collective-permute-start.2) | collective-permute-done | bytes 65568 | tf_op jit(solution)/shard_map/ppermute | solution.py:23
  118.5 4.7 %collective-permute-start.5 = (bf16[128,256]{0,1:T(8,128)(2,1)S(1)}, bf16[128,256]{0,1:T(8,128)(2,1)S(1)}, u32[]{:S(2)}, u32[]{:S(2)}) collective-permute-start(bf16[128,256]{0,1:T(8,128)(2,1)S(1)} %collective-permute-done.3), channel_id=1, source_target_pairs={{0,28},{4,0},{8,4},{12,8},{16,12},{20,16},{24,20},{28,24},{1,29},{... | collective-permute-start | bytes 196616 | tf_op jit(solution)/shard_map/ppermute | solution.py:28
  126.8 5.7 %collective-permute-done.6 = bf16[128,256]{0,1:T(8,128)(2,1)S(1)} collective-permute-done((bf16[128,256]{0,1:T(8,128)(2,1)S(1)}, bf16[128,256]{0,1:T(8,128)(2,1)S(1)}, u32[]{:S(2)}, u32[]{:S(2)}) %collective-permute-start.6) | collective-permute-done | bytes 65568 | tf_op jit(solution)/shard_map/ppermute | solution.py:23
  133.1 2.0 convolution_convert_fusion.1
  135.9 3.4 %fusion.36 = f32[256,512]{1,0:T(8,128)} fusion(bf16[256,2048]{1,0:T(8,128)(2,1)} %all-gather.2.cloned.1.call-done, bf16[2048,512]{1,0:T(8,128)(2,1)} %param.20), kind=kOutput, calls=%fused_computation.90 | convolution fusion | flops 536870912 | bytes 3670016 | tf_op jit(solution)/shard_map/dot_general | solution.py:88
  139.3 1.2 reshape.198
  144.4 1.9 copy.161
  146.3 1.1 fusion.34
  147.5 1.3 copy.145
  148.8 10.2 %fusion.2 = (f32[2,2,256]{2,1,0:T(2,128)S(1)}, f32[2,3840,256,2]{2,1,3,0:T(8,128)}) fusion(pred[256,3840]{0,1:T(8,128)(4,1)} %pad_add_fusion, bf16[256,2,2,64]{3,0,2,1:T(8,128)(2,1)} %bitcast.71, bf16[256,2,2,64]{3,0,2,1:T(8,128)(2,1)} %bitcast.72, bf16[2048,2,128]{2,0,1:T(8,128)(2,1)} %copy.145, bf16[256,2,128]{2,0,1:T(8,128)(2,1)S(1)} %maximum_convert_fusion, ...), kind=kOutput, calls=%fused_computation.4 | convolution fusion | flops 1026817024 | bytes 18944000 | tf_op jit(solution)/shard_map/tkgd,skd->kgts/dot_general | solution.py:165
  158.9 9.1 %fusion = f32[2,2,256]{2,1,0:T(2,128)S(1)} fusion(f32[2,3840,256,2]{2,1,3,0:T(8,128)} %get-tuple-element.41, f32[2,2,256]{2,1,0:T(2,128)S(1)} %get-tuple-element.40, pred[256,3840]{0,1:T(8,128)(4,1)} %pad_add_fusion), kind=kLoop, calls=%fused_computation.2 | loop fusion | flops 15727616 | bytes 16719872 | tf_op jit(solution)/shard_map/reduce_sum | solution.py:168
  168.1 1.3 pad_maximum_fusion
  169.4 7.7 %fusion.19 = bf16[256,2,2,128]{0,3,2,1:T(8,128)(2,1)S(1)} fusion(bf16[3840,2,128,1]{0,2,3,1:T(8,128)(2,1)S(1)} %bitcast.67, f32[2,3840,256,2]{2,1,3,0:T(8,128)} %get-tuple-element.41, f32[2,2,256]{2,1,0:T(2,128)S(1)} %get-tuple-element.40, pred[256,3840]{0,1:T(8,128)(4,1)S(1)} %copy-done.3, f32[256,2,2]{0,2,1:T(2,128)S(1)} %bitcast.80), kind=kOutput, calls=%fused_computation.22 | convolution fusion | flops 1022623744 | bytes 18948096 | tf_op jit(solution)/shard_map/kgts,skd->kgtd/dot_general | solution.py:169
  177.1 1.7 convolution_convert_fusion
  179.8 27.2 %reduce-scatter.2.cloned.1.call-done = bf16[64,2048]{1,0:T(8,128)(2,1)} async-done(((bf16[256,2048]{1,0:T(8,128)(2,1)}), bf16[64,2048]{1,0:T(8,128)(2,1)}) %reduce-scatter.2.cloned.1.call-update) | async-done | bytes 262160 | tf_op jit(solution)/shard_map/reduce_scatter | solution.py:177
  (90 shorter events, 28.0 us)
Async XLA Ops:
  7.2 169.9 %copy-start = (bf16[512,2048]{1,0:T(8,128)(2,1)S(1)}, bf16[512,2048]{1,0:T(8,128)(2,1)}, u32[]{:S(2)}) copy-start(bf16[512,2048]{1,0:T(8,128)(2,1)} %param.25) | copy-start | bytes 6291460
  7.2 24.7 %copy-start.10 = (s32[1,256]{1,0:T(1,128)S(1)}, s32[1,256]{1,0:T(1,128)}, u32[]{:S(2)}) copy-start(s32[1,256]{1,0:T(1,128)} %param.34) | copy-start | bytes 3076
  7.2 25.0 %copy-start.9 = (bf16[128,256]{1,0:T(8,128)(2,1)S(1)}, bf16[128,256]{1,0:T(8,128)(2,1)}, u32[]{:S(2)}) copy-start(bf16[128,256]{1,0:T(8,128)(2,1)} %param.26) | copy-start | bytes 196612
  8.9 76.5 %collective-permute-start = (bf16[128,256]{0,1:T(8,128)(2,1)}, bf16[128,256]{0,1:T(8,128)(2,1)}, u32[]{:S(2)}, u32[]{:S(2)}) collective-permute-start(bf16[128,256]{0,1:T(8,128)(2,1)} %copy.150), channel_id=1, source_target_pairs={{0,4},{4,8},{8,12},{12,16},{16,20},{20,24},{24,28},{28,0},{1,5},{5... | collective-permute-start | bytes 196616 | tf_op jit(solution)/shard_map/ppermute | solution.py:23
  11.9 75.4 %collective-permute-start.1 = (bf16[128,256]{0,1:T(8,128)(2,1)}, bf16[128,256]{0,1:T(8,128)(2,1)}, u32[]{:S(2)}, u32[]{:S(2)}) collective-permute-start(bf16[128,256]{0,1:T(8,128)(2,1)} %copy.150), channel_id=1, source_target_pairs={{0,28},{4,0},{8,4},{12,8},{16,12},{20,16},{24,20},{28,24},{1,29},{... | collective-permute-start | bytes 196616 | tf_op jit(solution)/shard_map/ppermute | solution.py:28
  17.3 58.1 %all-to-all-start = ((s32[8,1,1]{2,1,0:T(1,128)}), s32[8,1,1]{2,1,0:T(1,128)S(1)}, u32[]{:S(2)}, u32[]{:S(2)}) async-start(s32[8,1,1]{2,1,0:T(1,128)} %copy.139), calls=%async_computation | async-start | bytes 8192 | tf_op jit(solution)/shard_map/all_to_all | solution.py:134
  20.6 112.5 %all-gather.2.cloned.1.call-start = ((), (), s32[]{:S(2)}) async-start(), calls=%async_computation.3 | async-start | bytes 1310720 | tf_op jit(solution)/shard_map/all_gather | solution.py:85
  78.1 66.3 %all-to-all-start.1 = ((bf16[8,256,512]{1,2,0:T(8,128)(2,1)}), bf16[8,256,512]{1,2,0:T(8,128)(2,1)}, u32[]{:S(2)}, u32[]{:S(2)}) async-start(bf16[8,256,512]{1,2,0:T(8,128)(2,1)} %broadcast_select_fusion), calls=%async_computation.1 | async-start | bytes 4194304 | tf_op jit(solution)/shard_map/all_to_all | solution.py:142
  82.5 124.4 %reduce-scatter.2.cloned.1.call-start = ((), (), s32[]{:S(2)}) async-start(), calls=%async_computation.4 | async-start | bytes 1310720 | tf_op jit(solution)/shard_map/reduce_scatter | solution.py:177
  85.4 33.0 %collective-permute-start.2 = (bf16[128,256]{0,1:T(8,128)(2,1)}, bf16[128,256]{0,1:T(8,128)(2,1)S(1)}, u32[]{:S(2)}, u32[]{:S(2)}) collective-permute-start(bf16[128,256]{0,1:T(8,128)(2,1)} %collective-permute-done), channel_id=1, source_target_pairs={{0,4},{4,8},{8,12},{12,16},{16,20},{20,24},{24,28},{28,0},{1,5},{5... | collective-permute-start | bytes 196616 | tf_op jit(solution)/shard_map/ppermute | solution.py:23
  87.3 31.2 %collective-permute-start.3 = (bf16[128,256]{0,1:T(8,128)(2,1)}, bf16[128,256]{0,1:T(8,128)(2,1)S(1)}, u32[]{:S(2)}, u32[]{:S(2)}) collective-permute-start(bf16[128,256]{0,1:T(8,128)(2,1)} %collective-permute-done.1), channel_id=1, source_target_pairs={{0,28},{4,0},{8,4},{12,8},{16,12},{20,16},{24,20},{28,24},{1,29},{... | collective-permute-start | bytes 196616 | tf_op jit(solution)/shard_map/ppermute | solution.py:28
  118.5 7.1 %collective-permute-start.4 = (bf16[128,256]{0,1:T(8,128)(2,1)S(1)}, bf16[128,256]{0,1:T(8,128)(2,1)S(1)}, u32[]{:S(2)}, u32[]{:S(2)}) collective-permute-start(bf16[128,256]{0,1:T(8,128)(2,1)S(1)} %collective-permute-done.2), channel_id=1, source_target_pairs={{0,4},{4,8},{8,12},{12,16},{16,20},{20,24},{24,28},{28,0},{1,5},{5... | collective-permute-start | bytes 196616 | tf_op jit(solution)/shard_map/ppermute | solution.py:23
  118.5 7.7 %collective-permute-start.5 = (bf16[128,256]{0,1:T(8,128)(2,1)S(1)}, bf16[128,256]{0,1:T(8,128)(2,1)S(1)}, u32[]{:S(2)}, u32[]{:S(2)}) collective-permute-start(bf16[128,256]{0,1:T(8,128)(2,1)S(1)} %collective-permute-done.3), channel_id=1, source_target_pairs={{0,28},{4,0},{8,4},{12,8},{16,12},{20,16},{24,20},{28,24},{1,29},{... | collective-permute-start | bytes 196616 | tf_op jit(solution)/shard_map/ppermute | solution.py:28
  125.5 7.0 %collective-permute-start.6 = (bf16[128,256]{0,1:T(8,128)(2,1)S(1)}, bf16[128,256]{0,1:T(8,128)(2,1)S(1)}, u32[]{:S(2)}, u32[]{:S(2)}) collective-permute-start(bf16[128,256]{0,1:T(8,128)(2,1)S(1)} %collective-permute-done.4), channel_id=1, source_target_pairs={{0,4},{4,8},{8,12},{12,16},{16,20},{20,24},{24,28},{28,0},{1,5},{5... | collective-permute-start | bytes 196616 | tf_op jit(solution)/shard_map/ppermute | solution.py:23
  135.1 6.7 %copy-start.5 = (bf16[256,256]{1,0:T(8,128)(2,1)}, bf16[256,256]{1,0:T(8,128)(2,1)S(1)}, u32[]{:S(2)}) copy-start(bf16[256,256]{1,0:T(8,128)(2,1)S(1)} %convolution_convert_fusion.1) | copy-start | bytes 393220
  140.5 2.7 %copy-start.1 = (bf16[256,2048]{1,0:T(8,128)(2,1)S(1)}, bf16[256,2048]{1,0:T(8,128)(2,1)}, u32[]{:S(2)}) copy-start(bf16[256,2048]{1,0:T(8,128)(2,1)} %all-gather.2.cloned.1.call-done) | copy-start | bytes 3145732
  140.5 2.7 %copy-start.4 = (bf16[2048,256]{1,0:T(8,128)(2,1)S(1)}, bf16[2048,256]{1,0:T(8,128)(2,1)}, u32[]{:S(2)}) copy-start(bf16[2048,256]{1,0:T(8,128)(2,1)} %param.21) | copy-start | bytes 3145732
  144.4 4.4 %copy-start.7 = (bf16[256,2,128]{2,0,1:T(8,128)(2,1)}, bf16[256,2,128]{2,0,1:T(8,128)(2,1)S(1)}, u32[]{:S(2)}) copy-start(bf16[256,2,128]{2,0,1:T(8,128)(2,1)S(1)} %maximum_convert_fusion) | copy-start | bytes 393220
  158.9 9.1 %copy-start.2 = (bf16[2048,256]{0,1:T(8,128)(2,1)S(1)}, bf16[2048,256]{0,1:T(8,128)(2,1)}, u32[]{:S(2)}) copy-start(bf16[2048,256]{0,1:T(8,128)(2,1)} %get-tuple-element.27) | copy-start | bytes 3145732
  158.9 9.1 %copy-start.6 = (bf16[256,256]{0,1:T(8,128)(2,1)S(1)}, bf16[256,256]{0,1:T(8,128)(2,1)}, u32[]{:S(2)}) copy-start(bf16[256,256]{0,1:T(8,128)(2,1)} %copy.154) | copy-start | bytes 393220
  168.0 1.4 copy-start.3
  177.1 1.8 copy-start.8
Sparse Core Ops, SparseCore 0:
  24.4 18.1 all-gather.1
  179.0 27.8 reduce-scatter.1
